TPU v7x, 32 devices: a whole 2x2x4 slice. The times are simulated.
32 devices in a mesh: dp: 8 (over y, x, core), mp: 4 (over z).
Axes of the slice: x: 2, y: 2, z: 4, core: 2. Of those that a mesh axis runs over, the one named last changes fastest.
Arguments:
- activations: bfloat16 [1024, 8192], P('dp'), may hold values from -16 to 16
- out_grads: bfloat16 [1024, 16384], P('dp', 'mp'), may hold values from -1 to 1
- weight: float32 [8192, 16384], P('dp', 'mp'), may hold values from -16 to 16
- row_moment: float32 [8192], P('dp'), may hold values from 0.25 to 2
- col_moment: float32 [16384], P('mp'), may hold values from 0.25 to 2
Outputs:
- update: float32 [8192, 16384], P('dp', 'mp')
- new_rows: float32 [8192], P('dp')
- new_cols: float32 [16384], P('mp')
All inputs are finite; a program needn't handle non-finite values.
Results may differ from a plain program's by a relative error of at most 0.0003.
Values may be sent and summed in bfloat16 or wider, within the bound.
A program may use at most 128 MiB of HBM per device.

v0:
```python
import jax
import jax.numpy as jnp
from jax import lax
from jax.sharding import PartitionSpec as P

D = 8192
FF = 16384


BETA_TWO = 0.8
CLIP_LEVEL = 0.25
WEIGHT_DECAY = 0.1
EPSILON = 1e-06


def shards(activations, out_grads, weight, row_moment, col_moment):
    feature_rows = lax.all_to_all(activations, "dp", split_axis=1, concat_axis=0, tiled=True)
    weight_grad = lax.dot_general(
        feature_rows,
        lax.all_gather(out_grads, "dp", axis=0, tiled=True),
        (((0,), (0,)), ((), ())),
        preferred_element_type=jnp.float32,
    )
    squares = weight_grad * weight_grad
    row_total = lax.psum(jnp.sum(squares, axis=1), "mp")
    col_total = lax.psum(jnp.sum(squares, axis=0), "dp")
    new_rows = BETA_TWO * row_moment + (1.0 - BETA_TWO) * (row_total / FF)
    new_cols = BETA_TWO * col_moment + (1.0 - BETA_TWO) * (col_total / D)
    scaled = weight_grad / jnp.sqrt(new_rows[:, None] * new_cols[None, :])
    local_scaled = jnp.sum(scaled * scaled)
    local_weight = jnp.sum(weight * weight)
    scaled_sum, weight_sum = lax.psum((local_scaled, local_weight), ("dp", "mp"))
    factor = 1.0 / jnp.maximum(1.0, jnp.sqrt(scaled_sum / (D * FF)) / CLIP_LEVEL)
    direction = factor * scaled + WEIGHT_DECAY * weight
    direction_sum = lax.psum(jnp.sum(direction * direction), ("dp", "mp"))
    trust_ratio = jnp.sqrt(weight_sum / (direction_sum + EPSILON))
    return (trust_ratio * direction, new_rows, new_cols)


def solution(mesh):
    placed = (P("dp", None), P("dp", "mp"), P("dp", "mp"), P("dp"), P("mp"))
    return jax.shard_map(
        shards,
        mesh=mesh,
        in_specs=placed,
        out_specs=(P("dp", "mp"), P("dp"), P("mp")),
        check_vma=False,
    )
```

profile of v0, /device:TPU:0, one launch (start us, length us, event | category | flops | bytes accessed | tf_op | source)
XLA Modules:
  0.0 265.0 jit_solution(12759481528188188003)
XLA Ops:
  7.2 0.0 all-gather.2.cloned.1.call-start
  7.2 0.7 all-gather.2.cloned.1.call-update
  7.9 4.1 %copy.8 = bf16[128,8192]{0,1:T(8,128)(2,1)} copy(bf16[128,8192]{1,0:T(8,128)(2,1)} %param.5) | data formatting | bytes 4194304 | tf_op args[0]
  12.0 43.0 %all_to_all.19 = bf16[128,8,1024]{0,2,1:T(8,128)(2,1)S(1)} all-to-all(bf16[128,8,1024]{0,2,1:T(8,128)(2,1)} %bitcast.6), channel_id=1, replica_groups=mesh['dp'=8,'mp'=4] {'dp'}, dimensions={1} | all-to-all | bytes 4194304 | tf_op jit(solution)/shard_map/all_to_all | solution.py:17
  55.0 2.6 copy.9
  57.6 28.9 %all-gather.2.cloned.1.call-done = bf16[1024,4096]{1,0:T(8,128)(2,1)} async-done(((bf16[128,4096]{1,0:T(8,128)(2,1)}), bf16[1024,4096]{1,0:T(8,128)(2,1)}) %all-gather.2.cloned.1.call-update) | async-done | bytes 8388624 | tf_op jit(solution)/shard_map/all_gather | solution.py:20
  86.5 0.0 copy-start.3
  86.5 0.0 copy-start.2
  86.5 16.8 %multiply_reduce_fusion.4 = (f32[1024]{0:T(1024)S(1)}, f32[4096]{0:T(1024)S(1)}, f32[1024,4096]{1,0:T(8,128)}) fusion(bf16[1024,1024]{1,0:T(8,128)(2,1)} %bitcast.7, bf16[1024,4096]{1,0:T(8,128)(2,1)} %all-gather.2.cloned.1.call-done), kind=kOutput, calls=%fused_computation.6 | convolution fusion | flops 8602512384 | bytes 27283456 | tf_op jit(solution)/shard_map/dot_general | solution.py:18
  103.3 11.7 %psum.36 = f32[1024]{0:T(1024)S(1)} all-reduce(f32[1024]{0:T(1024)S(1)} %get-tuple-element.5), channel_id=1, replica_groups=mesh['dp'=8,'mp'=4] {'mp'}, use_global_device_ids=true, to_apply=%region_3.0 | all-reduce | flops 1024 | bytes 8192 | tf_op jit(solution)/shard_map/psum | solution.py:25
  114.9 22.3 %psum.37 = f32[4096]{0:T(1024)S(1)} all-reduce(f32[4096]{0:T(1024)S(1)} %get-tuple-element.6), channel_id=1, replica_groups=mesh['dp'=8,'mp'=4] {'dp'}, use_global_device_ids=true, to_apply=%region_5.0 | all-reduce | flops 4096 | bytes 32768 | tf_op jit(solution)/shard_map/psum | solution.py:26
  137.2 0.0 copy-done.3
  137.3 0.0 copy-done.2
  137.3 0.0 copy-start.1
  137.3 0.0 copy-start
  137.3 9.0 %multiply_reduce_fusion.1 = f32[]{:T(128)} fusion(f32[1024,4096]{1,0:T(8,128)} %get-tuple-element.9, f32[4096]{0:T(1024)S(1)} %multiply_add_fusion.1, f32[1024]{0:T(1024)S(1)} %multiply_add_fusion.2), kind=kLoop, calls=%fused_computation.2 | loop fusion | flops 16777215 | bytes 16797700 | tf_op jit(solution)/shard_map/reduce_sum | solution.py:30
  146.3 37.1 %psum.38 = f32[]{:T(128)} all-reduce(f32[]{:T(128)} %multiply_reduce_fusion.1), channel_id=1, replica_groups=mesh['dp'=8,'mp'=4] {'dp','mp'}, use_global_device_ids=true, to_apply=%region_7.0 | all-reduce | flops 1 | bytes 8 | tf_op jit(solution)/shard_map/psum | solution.py:32
  184.2 13.1 %multiply_reduce_fusion = (f32[]{:T(128)}, f32[]{:T(128)}) fusion(f32[1024,4096]{1,0:T(8,128)} %param.7, f32[1024,4096]{1,0:T(8,128)} %get-tuple-element.9, f32[4096]{0:T(1024)S(1)} %multiply_add_fusion.1, f32[1024]{0:T(1024)S(1)} %multiply_add_fusion.2, f32[]{:T(128)S(6)} %div.22), kind=kLoop, calls=%fused_computation | loop fusion | flops 37748736 | bytes 33574924 | tf_op jit(solution)/shard_map/reduce_sum | solution.py:35
  197.2 42.5 %all-reduce = (f32[]{:T(128)}, f32[]{:T(128)}) all-reduce(f32[]{:T(128)} %get-tuple-element.4, f32[]{:T(128)} %get-tuple-element.3), channel_id=1, replica_groups=mesh['dp'=8,'mp'=4] {'dp','mp'}, use_global_device_ids=true, to_apply=%region_1.0 | all-reduce | flops 2 | bytes 16 | tf_op jit(solution)/shard_map/psum | solution.py:32
  241.1 0.0 copy-done.1
  241.1 0.0 copy-done
  241.1 17.0 %broadcast_multiply_fusion = f32[1024,4096]{1,0:T(8,128)} fusion(f32[]{:T(128)S(6)} %sqrt.11, f32[1024,4096]{1,0:T(8,128)} %param.7, f32[1024,4096]{1,0:T(8,128)} %get-tuple-element.9, f32[4096]{0:T(1024)S(1)} %multiply_add_fusion.1, f32[1024]{0:T(1024)S(1)} %multiply_add_fusion.2, f32[]{:T(128)S(6)} %div.22), kind=kLoop, calls=%fused_computation.7 | loop fusion | flops 25165824 | bytes 50352136 | tf_op jit(solution)/shard_map/mul | solution.py:37
  (2 shorter events, 0.0 us)
Async XLA Ops:
  7.2 79.3 %all-gather.2.cloned.1.call-start = ((), (), s32[]{:S(2)}) async-start(), calls=%async_computation.1 | async-start | bytes 9437184 | tf_op jit(solution)/shard_map/all_gather | solution.py:20
  86.5 50.8 %copy-start.3 = (f32[1024]{0:T(1024)S(1)}, f32[1024]{0:T(1024)}, u32[]{:S(2)}) copy-start(f32[1024]{0:T(1024)} %param.8) | copy-start | bytes 12292
  86.5 50.8 %copy-start.2 = (f32[4096]{0:T(1024)S(1)}, f32[4096]{0:T(1024)}, u32[]{:S(2)}) copy-start(f32[4096]{0:T(1024)} %param.9) | copy-start | bytes 49156
  137.3 103.8 %copy-start.1 = (f32[1024]{0:T(1024)}, f32[1024]{0:T(1024)S(1)}, u32[]{:S(2)}) copy-start(f32[1024]{0:T(1024)S(1)} %multiply_add_fusion.2) | copy-start | bytes 12292
  137.3 103.8 %copy-start = (f32[4096]{0:T(1024)}, f32[4096]{0:T(1024)S(1)}, u32[]{:S(2)}) copy-start(f32[4096]{0:T(1024)S(1)} %multiply_add_fusion.1) | copy-start | bytes 49156
Sparse Core Ops, SparseCore 0:
  9.9 76.5 all-gather.1
where the time goes:
time: 266 us; the launch traced here: 265 us
  blocking collectives  157 us (59%)
  other arithmetic  39.1 us (15%)
  waiting for transfers between devices  29.5 us (11%)
  matrix products  16.8 us (6%)
  between operations  16.2 us (6%)
  local copies, waits for them, and re-layouts  6.73 us (3%)
    psum x2, blocking collectives, shards(): lax.psum((local_scaled, local_weight), ('dp', 'mp'))  79.6 us
    all_to_all x1, blocking collectives, shards(): lax.all_to_all(activations, 'dp', split_axis=1, concat_axis=0, tiled=True)  43 us
    all_gather x1, waiting for transfers between devices, shards(): lax.all_gather(out_grads, 'dp', axis=0, tiled=True)  28.9 us
    psum x1, blocking collectives, shards(): col_total = lax.psum(jnp.sum(squares, axis=0), 'dp')  22.3 us
    mul x1, other arithmetic, shards(): return (trust_ratio * direction, new_rows, new_cols)  17 us
    dot_general x1, matrix products, shards(): lax.dot_general(feature_rows, lax.all_gather(out_grads, 'dp', axis=0, til...  16.8 us
    reduce_sum x1, other arithmetic, shards(): direction_sum = lax.psum(jnp.sum(direction * direction), ('dp', 'mp'))  13.1 us
    psum x1, blocking collectives, shards(): row_total = lax.psum(jnp.sum(squares, axis=1), 'mp')  11.7 us
  transfers between devices with their start and end apart: 1, of which 1 were waited for; matrix products, arithmetic and copies ran while one was open for 3% of the time, Pallas kernels for 0%

commit v1 on v0

v1 whole, which is shorter than its diff:
```python
import functools
import math

import jax
import jax.numpy as jnp
from jax import lax
from jax.experimental import pallas as pl
from jax.experimental.pallas import tpu as pltpu
from jax.sharding import PartitionSpec as P

D = 8192
FF = 16384

BETA_TWO = 0.8
CLIP_LEVEL = 0.25
WEIGHT_DECAY = 0.1
EPSILON = 1e-06

MESH = pl.DeviceIdType.MESH
F32 = jnp.float32
BLOCKS = 4
SHARE = 2
LANES = 128


def grid_of(chips):
    wide = max(k for k in range(1, math.isqrt(chips) + 1) if chips % k == 0)
    return chips // wide, wide


def share_of(planes, tokens):
    share = 1
    while share * 2 <= SHARE and planes % (share * 2) == 0 and tokens % (share * 32) == 0:
        share *= 2
    return share


def reduce_kernel(
    ndp, nmp, share,
    act, og, weight, row_moment, col_moment,
    grad, held_weight, new_rows, new_cols, coefs,
    feat, feat_t, gbuf, row_acc, col_acc, row_slots, col_slots, row_scale, col_scale,
    sum_mp, sum_dp,
    local_sem, weight_sem,
    a_send, a_recv, ab_send, ab_recv, az_send, az_recv,
    ix_send, ix_recv, iy_send, iy_recv,
    jx_send, jx_recv, jy_send, jy_recv,
    o_send, o_recv, bx_send, bx_recv, by_send, by_recv,
    cx_send, cx_recv, cy_send, cy_recv,
    r_send, r_recv, c_send, c_recv, p_send, p_recv, q_send, q_recv,
):
    me = lax.axis_index("dp")
    plane = lax.axis_index("mp")
    chips = ndp // 2
    ny, nx = grid_of(chips)
    core = lax.rem(me, 2)
    chip = me // 2
    x = lax.rem(chip, nx)
    y = chip // nx
    sibling = me + 1 - 2 * core
    rows, cols = grad.shape
    tokens = ndp * gbuf.shape[2] * gbuf.shape[3]
    width = cols // BLOCKS
    part = lax.rem(plane, share)
    base = plane - part

    def index_of(yy, xx, cc):
        return (yy * nx + xx) * 2 + cc

    def x_at(k):
        return lax.rem(x + k + nx, nx)

    def y_at(k):
        return lax.rem(y + k + ny, ny)

    def at_dp(d):
        return {"dp": d, "mp": plane}

    def at_mp(z):
        return {"dp": me, "mp": z}

    sends = []

    def send(src, dst, send_sem, recv_sem, device):
        copy = pltpu.make_async_remote_copy(
            src_ref=src, dst_ref=dst, send_sem=send_sem, recv_sem=recv_sem,
            device_id=device, device_id_type=MESH,
        )
        copy.start()
        sends.append(copy)

    def arrived(ref, recv_sem, send_sem):
        pltpu.make_async_remote_copy(
            src_ref=ref, dst_ref=ref, send_sem=send_sem, recv_sem=recv_sem,
            device_id=at_dp(sibling), device_id_type=MESH,
        ).wait_recv()

    def feature_cols(d):
        return pl.ds(pl.multiple_of(d * rows, rows), rows)

    weight_rows = rows // 4
    weight_copies = [
        pltpu.make_async_copy(
            weight.at[pl.ds(i * weight_rows, weight_rows)],
            held_weight.at[pl.ds(i * weight_rows, weight_rows)],
            weight_sem.at[i],
        )
        for i in range(4)
    ]
    own_features = pltpu.make_async_copy(act.at[:, :, feature_cols(me)], feat.at[me], local_sem.at[BLOCKS])
    own_features.start()
    own_blocks = []
    for b in range(BLOCKS):
        own_blocks.append(
            pltpu.make_async_copy(og.at[:, :, pl.ds(b * width, width)], gbuf.at[b, me], local_sem.at[b])
        )
        own_blocks[b].start()

    barrier = pltpu.get_barrier_semaphore()
    for k in range(1, ndp):
        pl.semaphore_signal(barrier, inc=1, device_id=at_dp(lax.rem(me + k, ndp)), device_id_type=MESH)
    for k in range(1, nmp):
        pl.semaphore_signal(barrier, inc=1, device_id=at_mp(lax.rem(plane + k, nmp)), device_id_type=MESH)
    pl.semaphore_wait(barrier, ndp + nmp - 2)

    for k in range(1, chips):
        other = lax.rem(chip + k, chips)
        for c in range(2):
            there = 2 * other + c
            send(act.at[part, :, feature_cols(there)], feat.at[me, part], a_send.at[k, c], a_recv.at[k, core], at_dp(there))

    def half(h, b):
        return og.at[h, :, pl.ds(b * width, width)]

    def first_hops(b):
        for k in range(1, nx):
            send(half(0, b), gbuf.at[b, me, 0], ix_send.at[b, k], ix_recv.at[b, k], at_dp(index_of(y, x_at(k), core)))
        for k in range(1, ny):
            send(half(1, b), gbuf.at[b, me, 1], iy_send.at[b, k], iy_recv.at[b, k], at_dp(index_of(y_at(k), x, core)))

    first_hops(0)
    send(act.at[:, :, feature_cols(sibling)], feat.at[me], ab_send.at[0], ab_recv.at[0], at_dp(sibling))
    for copy in weight_copies:
        copy.start()
    first_hops(1)
    for b in range(BLOCKS):
        send(og.at[:, :, pl.ds(b * width, width)], gbuf.at[b, me], o_send.at[b], o_recv.at[b], at_dp(sibling))

    for k in range(1, chips):
        source = lax.rem(chip + chips - k, chips)
        for c in range(2):
            arrived(feat.at[2 * source + c, part], a_recv.at[k, c], a_send.at[k, c])
        for j in range(1, share):
            block = feat.at[pl.ds(2 * source, 2), part]
            send(block, block, az_send.at[k, j], az_recv.at[k, j], at_mp(base + lax.rem(part + j, share)))

    def second_hops(b):
        for j in range(nx):
            source = index_of(y, x_at(-j), core)
            block = gbuf.at[b, source, 0]
            if j:
                arrived(block, ix_recv.at[b, j], ix_send.at[b, j])
            for k in range(1, ny):
                send(half(0, b) if j == 0 else block, block, jy_send.at[b, j, k], jy_recv.at[b, j, k], at_dp(index_of(y_at(k), x, core)))
        for j in range(ny):
            source = index_of(y_at(-j), x, core)
            block = gbuf.at[b, source, 1]
            if j:
                arrived(block, iy_recv.at[b, j], iy_send.at[b, j])
            for k in range(1, nx):
                send(half(1, b) if j == 0 else block, block, jx_send.at[b, j, k], jx_recv.at[b, j, k], at_dp(index_of(y, x_at(k), core)))
        for j in range(1, nx):
            block = gbuf.at[b, index_of(y, x_at(-j), core), 0]
            send(block, block, bx_send.at[b, j], bx_recv.at[b, j], at_dp(sibling))
        for j in range(1, ny):
            block = gbuf.at[b, index_of(y_at(-j), x, core), 1]
            send(block, block, by_send.at[b, j], by_recv.at[b, j], at_dp(sibling))

    def to_sibling(b):
        for k in range(1, ny):
            for j in range(nx):
                block = gbuf.at[b, index_of(y_at(-k), x_at(-j), core), 0]
                arrived(block, jy_recv.at[b, j, k], jy_send.at[b, j, k])
                send(block, block, cy_send.at[b, j, k], cy_recv.at[b, j, k], at_dp(sibling))
        for k in range(1, nx):
            for j in range(ny):
                block = gbuf.at[b, index_of(y_at(-j), x_at(-k), core), 1]
                arrived(block, jx_recv.at[b, j, k], jx_send.at[b, j, k])
                send(block, block, cx_send.at[b, j, k], cx_recv.at[b, j, k], at_dp(sibling))

    def block_ready(b):
        other = 1 - core
        own_blocks[b].wait()
        arrived(gbuf.at[b, sibling], o_recv.at[b], o_send.at[b])
        for j in range(1, nx):
            arrived(gbuf.at[b, index_of(y, x_at(-j), other), 0], bx_recv.at[b, j], bx_send.at[b, j])
        for j in range(1, ny):
            arrived(gbuf.at[b, index_of(y_at(-j), x, other), 1], by_recv.at[b, j], by_send.at[b, j])
        for k in range(1, ny):
            for j in range(nx):
                arrived(gbuf.at[b, index_of(y_at(-k), x_at(-j), other), 0], cy_recv.at[b, j, k], cy_send.at[b, j, k])
        for k in range(1, nx):
            for j in range(ny):
                arrived(gbuf.at[b, index_of(y_at(-j), x_at(-k), other), 1], cx_recv.at[b, j, k], cx_send.at[b, j, k])

    def features_ready():
        own_features.wait()
        arrived(feat.at[sibling], ab_recv.at[0], ab_send.at[0])
        for k in range(1, chips):
            source = lax.rem(chip + chips - k, chips)
            for j in range(1, share):
                block = feat.at[pl.ds(2 * source, 2), lax.rem(part - j + share, share)]
                arrived(block, az_recv.at[k, j], az_send.at[k, j])
        shard = tokens // ndp
        for d in range(ndp):
            feat_t[:, d * shard:(d + 1) * shard] = feat[d].reshape(shard, rows).T

    tile = min(rows, 256)
    narrow = min(width, 512)

    def multiply(b):
        def body(i, carry):
            here = pl.ds(pl.multiple_of(i * tile, tile), tile)
            left = feat_t[here, :]
            for n in range(width // narrow):
                right = gbuf[b, :, :, :, n * narrow:(n + 1) * narrow].reshape(tokens, narrow)
                product = jnp.dot(left, right, preferred_element_type=F32)
                at = b * width + n * narrow
                grad[here, at:at + narrow] = product
                squares = product * product
                total = squares[:, :LANES]
                for l in range(1, narrow // LANES):
                    total = total + squares[:, l * LANES:(l + 1) * LANES]
                row_acc[here, :] += total
                col_acc[:, at:at + narrow] += jnp.sum(squares, axis=0, keepdims=True)
            return carry

        lax.fori_loop(0, rows // tile, body, 0)

    step = 32

    def weight_norm():
        for copy in weight_copies:
            copy.wait()

        def body(i, total):
            here = pl.ds(pl.multiple_of(i * step, step), step)
            for l in range(cols // LANES):
                piece = held_weight[here, l * LANES:(l + 1) * LANES]
                total = total + piece * piece
            return total

        return lax.fori_loop(0, rows // step, body, jnp.zeros((step, LANES), F32))

    row_acc[...] = jnp.zeros_like(row_acc)
    col_acc[...] = jnp.zeros_like(col_acc)

    second_hops(0)
    first_hops(2)
    weight_squares = weight_norm()
    second_hops(1)
    first_hops(3)
    to_sibling(0)
    second_hops(2)
    to_sibling(1)
    features_ready()
    block_ready(0)
    multiply(0)
    second_hops(3)
    to_sibling(2)
    block_ready(1)
    multiply(1)
    to_sibling(3)
    block_ready(2)
    multiply(2)
    block_ready(3)
    multiply(3)

    col_slots[me] = col_acc[...]
    for k in range(1, ndp):
        send(col_slots.at[me], col_slots.at[me], c_send.at[k], c_recv.at[k], at_dp(lax.rem(me + k, ndp)))
    row_slots[plane] = jnp.sum(row_acc[...].T, axis=0, keepdims=True)
    for k in range(1, nmp):
        send(row_slots.at[plane], row_slots.at[plane], r_send.at[k], r_recv.at[k], at_mp(lax.rem(plane + k, nmp)))
    for k in range(1, nmp):
        arrived(row_slots.at[lax.rem(plane + nmp - k, nmp)], r_recv.at[k], r_send.at[k])
    row_total = row_slots[0]
    for k in range(1, nmp):
        row_total = row_total + row_slots[k]
    rows_now = BETA_TWO * row_moment[...] + (1.0 - BETA_TWO) * (row_total / FF)
    new_rows[...] = rows_now
    row_scale[...] = jnp.broadcast_to(1.0 / jnp.sqrt(rows_now), (LANES, rows)).T
    for k in range(1, ndp):
        arrived(col_slots.at[lax.rem(me + ndp - k, ndp)], c_recv.at[k], c_send.at[k])
    col_total = col_slots[0]
    for k in range(1, ndp):
        col_total = col_total + col_slots[k]
    cols_now = BETA_TWO * col_moment[...] + (1.0 - BETA_TWO) * (col_total / D)
    new_cols[...] = cols_now
    col_scale[...] = 1.0 / jnp.sqrt(cols_now)

    def scale(i, totals):
        ss, sw = totals
        here = pl.ds(pl.multiple_of(i * step, step), step)
        by_row = row_scale[here, :]
        for l in range(cols // LANES):
            at = slice(l * LANES, (l + 1) * LANES)
            value = grad[here, at] * col_scale[:, at] * by_row
            grad[here, at] = value
            ss = ss + value * value
            sw = sw + value * held_weight[here, at]
        return ss, sw

    zero = jnp.zeros((step, LANES), F32)
    ss, sw = lax.fori_loop(0, rows // step, scale, (zero, zero))
    for i, total in enumerate((ss, sw, weight_squares)):
        sum_mp[plane, :, i * LANES:(i + 1) * LANES] = jnp.sum(total, axis=0, keepdims=True)
    for k in range(1, nmp):
        send(sum_mp.at[plane], sum_mp.at[plane], p_send.at[k], p_recv.at[k], at_mp(lax.rem(plane + k, nmp)))
    for k in range(1, nmp):
        arrived(sum_mp.at[lax.rem(plane + nmp - k, nmp)], p_recv.at[k], p_send.at[k])
    total = sum_mp[0]
    for k in range(1, nmp):
        total = total + sum_mp[k]
    sum_dp[me] = total
    for k in range(1, ndp):
        send(sum_dp.at[me], sum_dp.at[me], q_send.at[k], q_recv.at[k], at_dp(lax.rem(me + k, ndp)))
    for k in range(1, ndp):
        arrived(sum_dp.at[lax.rem(me + ndp - k, ndp)], q_recv.at[k], q_send.at[k])
    total = sum_dp[0]
    for k in range(1, ndp):
        total = total + sum_dp[k]
    scaled_sum, cross_sum, weight_sum = (
        jnp.broadcast_to(jnp.sum(total[:, i * LANES:(i + 1) * LANES], axis=1, keepdims=True), (1, LANES))
        for i in range(3)
    )
    factor = 1.0 / jnp.maximum(1.0, jnp.sqrt(scaled_sum / (D * FF)) / CLIP_LEVEL)
    direction_sum = (
        factor * factor * scaled_sum
        + (2.0 * WEIGHT_DECAY) * factor * cross_sum
        + (WEIGHT_DECAY * WEIGHT_DECAY) * weight_sum
    )
    trust_ratio = jnp.sqrt(weight_sum / (jnp.maximum(direction_sum, 0.0) + EPSILON))
    coefs[0:1, :] = trust_ratio * factor
    coefs[1:2, :] = trust_ratio * WEIGHT_DECAY
    for copy in sends:
        copy.wait_send()


def update_kernel(scaled, weight, coefs, out):
    rows, cols = out.shape
    here = pl.ds(pl.multiple_of(pl.program_id(0) * rows, rows), rows)
    by_scaled = coefs[0:1, :]
    by_weight = coefs[1:2, :]
    for l in range(cols // LANES):
        at = slice(l * LANES, (l + 1) * LANES)
        out[:, at] = by_scaled * scaled[here, at] + by_weight * weight[here, at]


def shards(ndp, nmp, activations, out_grads, weight, row_moment, col_moment):
    shard = activations.shape[0]
    rows, cols = weight.shape
    tokens = ndp * shard
    width = cols // BLOCKS
    chips = ndp // 2
    ny, nx = grid_of(chips)
    share = share_of(nmp, shard)
    part = shard // share
    vmem = pl.BlockSpec(memory_space=pltpu.VMEM)
    hbm = pl.BlockSpec(memory_space=pl.ANY)
    dma = pltpu.SemaphoreType.DMA

    def pair(*shape):
        return [dma(shape), dma(shape)]

    grad, held_weight, new_rows, new_cols, coefs = pl.pallas_call(
        functools.partial(reduce_kernel, ndp, nmp, share),
        out_shape=[
            pltpu.VMEM((rows, cols), F32),
            pltpu.VMEM((rows, cols), F32),
            jax.ShapeDtypeStruct((1, rows), F32),
            jax.ShapeDtypeStruct((1, cols), F32),
            pltpu.VMEM((2, LANES), F32),
        ],
        in_specs=[hbm, hbm, hbm, vmem, vmem],
        out_specs=[vmem] * 5,
        scratch_shapes=[
            pltpu.VMEM((ndp, share, part, rows), jnp.bfloat16),
            pltpu.VMEM((rows, tokens), jnp.bfloat16),
            pltpu.VMEM((BLOCKS, ndp, 2, shard // 2, width), jnp.bfloat16),
            pltpu.VMEM((rows, LANES), F32),
            pltpu.VMEM((1, cols), F32),
            pltpu.VMEM((nmp, 1, rows), F32),
            pltpu.VMEM((ndp, 1, cols), F32),
            pltpu.VMEM((rows, LANES), F32),
            pltpu.VMEM((1, cols), F32),
            pltpu.VMEM((nmp, 1, 3 * LANES), F32),
            pltpu.VMEM((ndp, 1, 3 * LANES), F32),
            dma((BLOCKS + 1,)),
            dma((4,)),
            *pair(chips, 2), *pair(1), *pair(chips, share),
            *pair(BLOCKS, nx), *pair(BLOCKS, ny),
            *pair(BLOCKS, ny, nx), *pair(BLOCKS, nx, ny),
            *pair(BLOCKS), *pair(BLOCKS, nx), *pair(BLOCKS, ny),
            *pair(BLOCKS, ny, nx), *pair(BLOCKS, nx, ny),
            *pair(nmp), *pair(ndp), *pair(nmp), *pair(ndp),
        ],
        compiler_params=pltpu.CompilerParams(
            collective_id=0, has_side_effects=True, vmem_limit_bytes=22 * 2**20
        ),
        cost_estimate=pl.CostEstimate(
            flops=2 * rows * cols * tokens, bytes_accessed=8 * rows * cols, transcendentals=0
        ),
        name="gradient",
    )(
        activations.reshape(share, part, ndp * rows),
        out_grads.reshape(2, shard // 2, cols),
        weight,
        row_moment.reshape(1, rows),
        col_moment.reshape(1, cols),
    )
    tile = min(rows, 128)
    update = pl.pallas_call(
        update_kernel,
        out_shape=jax.ShapeDtypeStruct((rows, cols), F32),
        grid=(rows // tile,),
        in_specs=[vmem, vmem, vmem],
        out_specs=pl.BlockSpec((tile, cols), lambda i: (i, 0)),
        compiler_params=pltpu.CompilerParams(vmem_limit_bytes=12 * 2**20),
        cost_estimate=pl.CostEstimate(flops=3 * rows * cols, bytes_accessed=4 * rows * cols, transcendentals=0),
        name="update",
    )(
        pltpu.with_memory_space_constraint(grad, pltpu.VMEM),
        pltpu.with_memory_space_constraint(held_weight, pltpu.VMEM),
        pltpu.with_memory_space_constraint(coefs, pltpu.VMEM),
    )
    return update, new_rows.reshape(rows), new_cols.reshape(cols)


def solution(mesh):
    placed = (P("dp", None), P("dp", "mp"), P("dp", "mp"), P("dp"), P("mp"))
    return jax.shard_map(
        functools.partial(shards, mesh.shape["dp"], mesh.shape["mp"]),
        mesh=mesh,
        in_specs=placed,
        out_specs=(P("dp", "mp"), P("dp"), P("mp")),
        check_vma=False,
    )
```

time: 266 us -> 109 us (0.41)
  blocking collectives: 157 us -> 0 us
  Pallas kernels: 0 us -> 83.6 us
  other arithmetic: 39.1 us -> 0 us
  waiting for transfers between devices: 29.5 us -> 0 us
  local copies, waits for them, and re-layouts: 6.73 us -> 24.6 us
  matrix products: 16.8 us -> 0 us
  between operations: 16.2 us -> 0.65 us
    psum x4 -> x0, blocking collectives: 114 us -> none  [the longest x2 79.6 us: shards(): lax.psum((local_scaled, local_weight), ('dp', 'mp'))]
    pallas_call x0 -> x2, Pallas kernels: none -> 83.6 us  [the longest x1 76.5 us: shards(): pl.pallas_call(functools.partial(reduce_kernel, ndp, nmp, share), out_sha...]
    all_to_all x1 -> x0, blocking collectives: 43 us -> none  [shards(): lax.all_to_all(activations, 'dp', split_axis=1, concat_axis=0, tiled=True)]
    all_gather x1 -> x0, waiting for transfers between devices: 28.9 us -> none  [shards(): lax.all_gather(out_grads, 'dp', axis=0, tiled=True)]
    reduce_sum x2 -> x0, other arithmetic: 22.1 us -> none  [the longest x1 13.1 us: shards(): direction_sum = lax.psum(jnp.sum(direction * direction), ('dp', 'mp'))]
    unnamed x9 -> x14, local copies, waits for them, and re-layouts: 4.09 us -> 24.6 us
    mul x1 -> x0, other arithmetic: 17 us -> none  [shards(): return (trust_ratio * direction, new_rows, new_cols)]
    dot_general x1 -> x0, matrix products: 16.8 us -> none  [shards(): lax.dot_general(feature_rows, lax.all_gather(out_grads, 'dp', axis=0, til...]
  transfers between devices with their start and end apart: 1 -> 0, of which waited for: 1 -> 0; matrix products, arithmetic and copies ran while one was open for 3% -> 0% of each run, Pallas kernels for 0% -> 0%
where the time goes in v1:
time: 109 us
  Pallas kernels  83.6 us (77%)
  local copies, waits for them, and re-layouts  24.6 us (23%)
    pallas_call x1, Pallas kernels, shards(): pl.pallas_call(functools.partial(reduce_kernel, ndp, nmp, share), out_sha...  76.5 us
    unnamed x14, local copies, waits for them, and re-layouts  24.6 us
    pallas_call x1, Pallas kernels, shards(): pl.pallas_call(update_kernel, out_shape=jax.ShapeDtypeStruct((rows, cols)...  7.14 us

profile of v1, /device:TPU:0, one launch (start us, length us, event | category | flops | bytes accessed | tf_op | source)
XLA Modules:
  0.0 108.9 jit_solution(13070092831641262117)
XLA Ops:
  0.6 76.5 %gradient.1 = (f32[1024,4096]{1,0:T(8,128)S(1)}, f32[1024,4096]{1,0:T(8,128)S(1)}, f32[1,1024]{1,0:T(1,128)}, f32[1,4096]{1,0:T(1,128)}, f32[2,128]{1,0:T(2,128)S(1)}) custom-call(bf16[2,64,8192]{2,1,0:T(8,128)(2,1)} %bitcast.8, bf16[2,64,4096]{2,1,0:T(8,128)(2,1)} %bitcast.9, f32[1024,4096]{1,0:T(8,128)} %weight.1, f32[1,1024]{1,0:T(1,128)} %bitcast.11, ...), custom_call_target="tpu_custom_call" | custom-call | flops 8589934592 | bytes 33554432 | tf_op jit(solution)/shard_map/gradient/pallas_call | solution.py:376
  77.1 0.0 copy-start
  77.2 6.2 %copy-done = f32[1024,4096]{1,0:T(8,128)} copy-done((f32[1024,4096]{1,0:T(8,128)}, f32[1024,4096]{1,0:T(8,128)S(1)}, u32[]{:S(2)}) %copy-start) | copy-done | bytes 16777240
  83.3 0.0 copy-start.2
  83.3 5.7 %copy-done.2 = f32[1024,4096]{1,0:T(8,128)} copy-done((f32[1024,4096]{1,0:T(8,128)}, f32[1024,4096]{1,0:T(8,128)S(1)}, u32[]{:S(2)}) %copy-start.2) | copy-done | bytes 16777240
  89.0 0.0 copy-start.1
  89.0 5.8 %copy-done.1 = f32[1024,4096]{1,0:T(8,128)S(1)} copy-done((f32[1024,4096]{1,0:T(8,128)S(1)}, f32[1024,4096]{1,0:T(8,128)}, u32[]{:S(2)}) %copy-start.1) | copy-done | bytes 16777240
  94.8 0.0 copy-start.3
  94.8 5.8 %copy-done.3 = f32[1024,4096]{1,0:T(8,128)S(1)} copy-done((f32[1024,4096]{1,0:T(8,128)S(1)}, f32[1024,4096]{1,0:T(8,128)}, u32[]{:S(2)}) %copy-start.3) | copy-done | bytes 16777240
  100.6 0.0 copy-start.5
  100.6 0.0 copy-start.4
  100.6 7.1 %update.1 = f32[1024,4096]{1,0:T(8,128)} custom-call(f32[1024,4096]{1,0:T(8,128)S(1)} %copy-done.1, f32[1024,4096]{1,0:T(8,128)S(1)} %copy-done.3, f32[2,128]{1,0:T(2,128)S(1)} %get-tuple-element.10.coefs), custom_call_target="tpu_custom_call" | custom-call | flops 12582912 | bytes 16777216 | tf_op jit(solution)/shard_map/update/pallas_call | solution.py:423
  107.7 0.0 copy-done.5
  107.7 0.6 copy.10
  108.3 0.0 copy-done.4
  108.3 0.6 copy.11
Async XLA Ops:
  77.1 6.2 %copy-start = (f32[1024,4096]{1,0:T(8,128)}, f32[1024,4096]{1,0:T(8,128)S(1)}, u32[]{:S(2)}) copy-start(f32[1024,4096]{1,0:T(8,128)S(1)} %get-tuple-element.8.scaled) | copy-start | bytes 50331652
  83.3 5.7 %copy-start.2 = (f32[1024,4096]{1,0:T(8,128)}, f32[1024,4096]{1,0:T(8,128)S(1)}, u32[]{:S(2)}) copy-start(f32[1024,4096]{1,0:T(8,128)S(1)} %get-tuple-element.9.weight) | copy-start | bytes 50331652
  89.0 5.8 %copy-start.1 = (f32[1024,4096]{1,0:T(8,128)S(1)}, f32[1024,4096]{1,0:T(8,128)}, u32[]{:S(2)}) copy-start(f32[1024,4096]{1,0:T(8,128)} %copy-done) | copy-start | bytes 50331652
  94.8 5.8 %copy-start.3 = (f32[1024,4096]{1,0:T(8,128)S(1)}, f32[1024,4096]{1,0:T(8,128)}, u32[]{:S(2)}) copy-start(f32[1024,4096]{1,0:T(8,128)} %copy-done.2) | copy-start | bytes 50331652
  100.6 7.1 %copy-start.5 = (f32[1,1024]{1,0:T(1,128)S(1)}, f32[1,1024]{1,0:T(1,128)}, u32[]{:S(2)}) copy-start(f32[1,1024]{1,0:T(1,128)} %get-tuple-element.11) | copy-start | bytes 12292
  100.6 7.7 %copy-start.4 = (f32[1,4096]{1,0:T(1,128)S(1)}, f32[1,4096]{1,0:T(1,128)}, u32[]{:S(2)}) copy-start(f32[1,4096]{1,0:T(1,128)} %get-tuple-element.12) | copy-start | bytes 49156

commit v2 on v1

--- a/solution.py
+++ b/solution.py
@@ -18,7 +18,9 @@
 
 MESH = pl.DeviceIdType.MESH
 F32 = jnp.float32
-BLOCKS = 4
+BLOCKS = 8
+READY = 5
+GRANT = 22 * 2**20
 SHARE = 2
 LANES = 128
 
@@ -38,9 +40,8 @@
 def reduce_kernel(
     ndp, nmp, share,
     act, og, weight, row_moment, col_moment,
-    grad, held_weight, new_rows, new_cols, coefs,
-    feat, feat_t, gbuf, row_acc, col_acc, row_slots, col_slots, row_scale, col_scale,
-    sum_mp, sum_dp,
+    grad, held_weight, row_scale, new_rows, new_cols, coefs,
+    feat, feat_t, gbuf, row_acc, ss_acc, sw_acc, row_slots, col_slots, sum_mp, sum_dp,
     local_sem, weight_sem,
     a_send, a_recv, ab_send, ab_recv, az_send, az_recv,
     ix_send, ix_recv, iy_send, iy_recv,
@@ -219,23 +220,55 @@
     narrow = min(width, 512)
 
     def multiply(b):
-        def body(i, carry):
+        block_ready(b)
+
+        def body(i, total):
             here = pl.ds(pl.multiple_of(i * tile, tile), tile)
             left = feat_t[here, :]
+            parts = []
             for n in range(width // narrow):
                 right = gbuf[b, :, :, :, n * narrow:(n + 1) * narrow].reshape(tokens, narrow)
                 product = jnp.dot(left, right, preferred_element_type=F32)
                 at = b * width + n * narrow
                 grad[here, at:at + narrow] = product
                 squares = product * product
-                total = squares[:, :LANES]
+                across = squares[:, :LANES]
                 for l in range(1, narrow // LANES):
-                    total = total + squares[:, l * LANES:(l + 1) * LANES]
-                row_acc[here, :] += total
-                col_acc[:, at:at + narrow] += jnp.sum(squares, axis=0, keepdims=True)
+                    across = across + squares[:, l * LANES:(l + 1) * LANES]
+                row_acc[here, :] += across
+                parts.append(jnp.sum(squares, axis=0, keepdims=True))
+            return total + (parts[0] if len(parts) == 1 else jnp.concatenate(parts, axis=1))
+
+        col_slots[b, me] = lax.fori_loop(0, rows // tile, body, jnp.zeros((1, width), F32))
+        for k in range(1, ndp):
+            send(col_slots.at[b, me], col_slots.at[b, me], c_send.at[b, k], c_recv.at[b, k], at_dp(lax.rem(me + k, ndp)))
+
+    def scale(b):
+        for k in range(1, ndp):
+            arrived(col_slots.at[b, lax.rem(me + ndp - k, ndp)], c_recv.at[b, k], c_send.at[b, k])
+        col_total = col_slots[b, 0]
+        for k in range(1, ndp):
+            col_total = col_total + col_slots[b, k]
+        block = slice(b * width, (b + 1) * width)
+        cols_now = BETA_TWO * col_moment[:, block] + (1.0 - BETA_TWO) * (col_total / D)
+        new_cols[:, block] = cols_now
+        by_col = 1.0 / jnp.sqrt(cols_now)
+
+        def body(i, carry):
+            here = pl.ds(pl.multiple_of(i * step, step), step)
+            ss = ss_acc[here, :]
+            sw = sw_acc[here, :]
+            for l in range(width // LANES):
+                at = slice(b * width + l * LANES, b * width + (l + 1) * LANES)
+                value = grad[here, at] * by_col[:, l * LANES:(l + 1) * LANES]
+                grad[here, at] = value
+                ss = ss + value * value
+                sw = sw + value * held_weight[here, at]
+            ss_acc[here, :] = ss
+            sw_acc[here, :] = sw
             return carry
 
-        lax.fori_loop(0, rows // tile, body, 0)
+        lax.fori_loop(0, rows // step, body, 0)
 
     step = 32
 
@@ -252,36 +285,38 @@
 
         return lax.fori_loop(0, rows // step, body, jnp.zeros((step, LANES), F32))
 
-    row_acc[...] = jnp.zeros_like(row_acc)
-    col_acc[...] = jnp.zeros_like(col_acc)
-
-    second_hops(0)
-    first_hops(2)
-    weight_squares = weight_norm()
-    second_hops(1)
-    first_hops(3)
-    to_sibling(0)
-    second_hops(2)
-    to_sibling(1)
-    features_ready()
-    block_ready(0)
-    multiply(0)
-    second_hops(3)
-    to_sibling(2)
-    block_ready(1)
-    multiply(1)
-    to_sibling(3)
-    block_ready(2)
-    multiply(2)
-    block_ready(3)
-    multiply(3)
-
-    col_slots[me] = col_acc[...]
-    for k in range(1, ndp):
-        send(col_slots.at[me], col_slots.at[me], c_send.at[k], c_recv.at[k], at_dp(lax.rem(me + k, ndp)))
+    for acc in (row_acc, ss_acc, sw_acc):
+        acc[...] = jnp.zeros_like(acc)
+    multiplied = scaled = 0
+    for b in range(BLOCKS):
+        second_hops(b)
+        if b + 2 < BLOCKS:
+            first_hops(b + 2)
+        if b == 0:
+            weight_squares = weight_norm()
+        else:
+            to_sibling(b - 1)
+        if b == READY:
+            features_ready()
+        if b >= READY:
+            for _ in range(2):
+                multiply(multiplied)
+                multiplied += 1
+            while scaled < multiplied - 2:
+                scale(scaled)
+                scaled += 1
+    while multiplied < BLOCKS - 1:
+        multiply(multiplied)
+        multiplied += 1
+    to_sibling(BLOCKS - 1)
+    multiply(BLOCKS - 1)
+
     row_slots[plane] = jnp.sum(row_acc[...].T, axis=0, keepdims=True)
     for k in range(1, nmp):
         send(row_slots.at[plane], row_slots.at[plane], r_send.at[k], r_recv.at[k], at_mp(lax.rem(plane + k, nmp)))
+    while scaled < BLOCKS - 1:
+        scale(scaled)
+        scaled += 1
     for k in range(1, nmp):
         arrived(row_slots.at[lax.rem(plane + nmp - k, nmp)], r_recv.at[k], r_send.at[k])
     row_total = row_slots[0]
@@ -290,29 +325,16 @@
     rows_now = BETA_TWO * row_moment[...] + (1.0 - BETA_TWO) * (row_total / FF)
     new_rows[...] = rows_now
     row_scale[...] = jnp.broadcast_to(1.0 / jnp.sqrt(rows_now), (LANES, rows)).T
-    for k in range(1, ndp):
-        arrived(col_slots.at[lax.rem(me + ndp - k, ndp)], c_recv.at[k], c_send.at[k])
-    col_total = col_slots[0]
-    for k in range(1, ndp):
-        col_total = col_total + col_slots[k]
-    cols_now = BETA_TWO * col_moment[...] + (1.0 - BETA_TWO) * (col_total / D)
-    new_cols[...] = cols_now
-    col_scale[...] = 1.0 / jnp.sqrt(cols_now)
-
-    def scale(i, totals):
+    scale(BLOCKS - 1)
+
+    def weigh(i, totals):
         ss, sw = totals
         here = pl.ds(pl.multiple_of(i * step, step), step)
         by_row = row_scale[here, :]
-        for l in range(cols // LANES):
-            at = slice(l * LANES, (l + 1) * LANES)
-            value = grad[here, at] * col_scale[:, at] * by_row
-            grad[here, at] = value
-            ss = ss + value * value
-            sw = sw + value * held_weight[here, at]
-        return ss, sw
+        return ss + ss_acc[here, :] * (by_row * by_row), sw + sw_acc[here, :] * by_row
 
     zero = jnp.zeros((step, LANES), F32)
-    ss, sw = lax.fori_loop(0, rows // step, scale, (zero, zero))
+    ss, sw = lax.fori_loop(0, rows // step, weigh, (zero, zero))
     for i, total in enumerate((ss, sw, weight_squares)):
         sum_mp[plane, :, i * LANES:(i + 1) * LANES] = jnp.sum(total, axis=0, keepdims=True)
     for k in range(1, nmp):
@@ -347,14 +369,19 @@
         copy.wait_send()
 
 
-def update_kernel(scaled, weight, coefs, out):
+def update_kernel(scaled, weight, row_scale, coefs, rows_in, cols_in, out, rows_out, cols_out):
     rows, cols = out.shape
     here = pl.ds(pl.multiple_of(pl.program_id(0) * rows, rows), rows)
-    by_scaled = coefs[0:1, :]
+    by_row = row_scale[here, :] * coefs[0:1, :]
     by_weight = coefs[1:2, :]
     for l in range(cols // LANES):
         at = slice(l * LANES, (l + 1) * LANES)
-        out[:, at] = by_scaled * scaled[here, at] + by_weight * weight[here, at]
+        out[:, at] = by_row * scaled[here, at] + by_weight * weight[here, at]
+
+    @pl.when(pl.program_id(0) == 0)
+    def _():
+        rows_out[...] = rows_in[...]
+        cols_out[...] = cols_in[...]
 
 
 def shards(ndp, nmp, activations, out_grads, weight, row_moment, col_moment):
@@ -373,27 +400,27 @@
     def pair(*shape):
         return [dma(shape), dma(shape)]
 
-    grad, held_weight, new_rows, new_cols, coefs = pl.pallas_call(
+    held = pl.pallas_call(
         functools.partial(reduce_kernel, ndp, nmp, share),
         out_shape=[
             pltpu.VMEM((rows, cols), F32),
             pltpu.VMEM((rows, cols), F32),
-            jax.ShapeDtypeStruct((1, rows), F32),
-            jax.ShapeDtypeStruct((1, cols), F32),
+            pltpu.VMEM((rows, LANES), F32),
+            pltpu.VMEM((1, rows), F32),
+            pltpu.VMEM((1, cols), F32),
             pltpu.VMEM((2, LANES), F32),
         ],
         in_specs=[hbm, hbm, hbm, vmem, vmem],
-        out_specs=[vmem] * 5,
+        out_specs=[vmem] * 6,
         scratch_shapes=[
             pltpu.VMEM((ndp, share, part, rows), jnp.bfloat16),
             pltpu.VMEM((rows, tokens), jnp.bfloat16),
             pltpu.VMEM((BLOCKS, ndp, 2, shard // 2, width), jnp.bfloat16),
             pltpu.VMEM((rows, LANES), F32),
-            pltpu.VMEM((1, cols), F32),
+            pltpu.VMEM((rows, LANES), F32),
+            pltpu.VMEM((rows, LANES), F32),
             pltpu.VMEM((nmp, 1, rows), F32),
-            pltpu.VMEM((ndp, 1, cols), F32),
-            pltpu.VMEM((rows, LANES), F32),
-            pltpu.VMEM((1, cols), F32),
+            pltpu.VMEM((BLOCKS, ndp, 1, width), F32),
             pltpu.VMEM((nmp, 1, 3 * LANES), F32),
             pltpu.VMEM((ndp, 1, 3 * LANES), F32),
             dma((BLOCKS + 1,)),
@@ -403,10 +430,10 @@
             *pair(BLOCKS, ny, nx), *pair(BLOCKS, nx, ny),
             *pair(BLOCKS), *pair(BLOCKS, nx), *pair(BLOCKS, ny),
             *pair(BLOCKS, ny, nx), *pair(BLOCKS, nx, ny),
-            *pair(nmp), *pair(ndp), *pair(nmp), *pair(ndp),
+            *pair(nmp), *pair(BLOCKS, ndp), *pair(nmp), *pair(ndp),
         ],
         compiler_params=pltpu.CompilerParams(
-            collective_id=0, has_side_effects=True, vmem_limit_bytes=22 * 2**20
+            collective_id=0, has_side_effects=True, vmem_limit_bytes=GRANT
         ),
         cost_estimate=pl.CostEstimate(
             flops=2 * rows * cols * tokens, bytes_accessed=8 * rows * cols, transcendentals=0
@@ -419,20 +446,27 @@
         row_moment.reshape(1, rows),
         col_moment.reshape(1, cols),
     )
-    tile = min(rows, 128)
-    update = pl.pallas_call(
+    tile = min(rows, 64)
+    whole = lambda i: (0, 0)
+    update, new_rows, new_cols = pl.pallas_call(
         update_kernel,
-        out_shape=jax.ShapeDtypeStruct((rows, cols), F32),
+        out_shape=[
+            jax.ShapeDtypeStruct((rows, cols), F32),
+            jax.ShapeDtypeStruct((1, rows), F32),
+            jax.ShapeDtypeStruct((1, cols), F32),
+        ],
         grid=(rows // tile,),
-        in_specs=[vmem, vmem, vmem],
-        out_specs=pl.BlockSpec((tile, cols), lambda i: (i, 0)),
-        compiler_params=pltpu.CompilerParams(vmem_limit_bytes=12 * 2**20),
+        in_specs=[vmem, vmem, vmem, vmem, vmem, vmem],
+        out_specs=[
+            pl.BlockSpec((tile, cols), lambda i: (i, 0)),
+            pl.BlockSpec((1, rows), whole),
+            pl.BlockSpec((1, cols), whole),
+        ],
+        compiler_params=pltpu.CompilerParams(vmem_limit_bytes=GRANT),
         cost_estimate=pl.CostEstimate(flops=3 * rows * cols, bytes_accessed=4 * rows * cols, transcendentals=0),
         name="update",
     )(
-        pltpu.with_memory_space_constraint(grad, pltpu.VMEM),
-        pltpu.with_memory_space_constraint(held_weight, pltpu.VMEM),
-        pltpu.with_memory_space_constraint(coefs, pltpu.VMEM),
+        *(pltpu.with_memory_space_constraint(held[i], pltpu.VMEM) for i in (0, 1, 2, 5, 3, 4))
     )
     return update, new_rows.reshape(rows), new_cols.reshape(cols)
 

time: 109 us -> 89.8 us (0.82)
  local copies, waits for them, and re-layouts: 24.6 us -> 0 us
  Pallas kernels: 83.6 us -> 88.9 us
    unnamed x14 -> x0, local copies, waits for them, and re-layouts: 24.6 us -> none
    pallas_call x1, Pallas kernels: 76.5 us -> 79.8 us  [shards(): pl.pallas_call(functools.partial(reduce_kernel, ndp, nmp, share), out_sha...]
    pallas_call x1, Pallas kernels: 7.14 us -> 9.07 us  [shards(): pl.pallas_call(update_kernel, out_shape=[jax.ShapeDtypeStruct((rows, cols...]
where the time goes in v2:
time: 89.8 us; the launch traced here: 89.5 us
  Pallas kernels  88.9 us (99%)
    pallas_call x1, Pallas kernels, shards(): pl.pallas_call(functools.partial(reduce_kernel, ndp, nmp, share), out_sha...  79.8 us
    pallas_call x1, Pallas kernels, shards(): pl.pallas_call(update_kernel, out_shape=[jax.ShapeDtypeStruct((rows, cols...  9.07 us

profile of v2, /device:TPU:0, one launch (start us, length us, event | category | flops | bytes accessed | tf_op | source)
XLA Modules:
  0.0 89.5 jit_solution(2597840875458304052)
XLA Ops:
  0.6 79.8 %gradient.1 = (f32[1024,4096]{1,0:T(8,128)S(1)}, f32[1024,4096]{1,0:T(8,128)S(1)}, f32[1024,128]{1,0:T(8,128)S(1)}, f32[1,1024]{1,0:T(1,128)S(1)}, f32[1,4096]{1,0:T(1,128)S(1)}, /*index=5*/f32[2,128]{1,0:T(2,128)S(1)}) custom-call(bf16[2,64,8192]{2,1,0:T(8,128)(2,1)} %bitcast.6, bf16[2,64,4096]{2,1,0:T(8,128)(2,1)} %bitcast.7, f32[1024,4096]{1,0:T(8,128)} %weight.1, ...), custom_call_target="tpu_custom_call" | custom-call | flops 8589934592 | bytes 33554432 | tf_op jit(solution)/shard_map/gradient/pallas_call | solution.py:403
  80.5 9.1 %update.1 = (f32[1024,4096]{1,0:T(8,128)}, f32[1,1024]{1,0:T(1,128)}, f32[1,4096]{1,0:T(1,128)}) custom-call(f32[1024,4096]{1,0:T(8,128)S(1)} %get-tuple-element.12.scaled, f32[1024,4096]{1,0:T(8,128)S(1)} %get-tuple-element.13.weight, f32[1024,128]{1,0:T(8,128)S(1)} %get-tuple-element.14.row_scale, f32[2,128]{1,0:T(2,128)S(1)} %get-tuple-element.15.coefs, ...), custom_call_target="tpu_custom_call" | custom-call | flops 12582912 | bytes 16777216 | tf_op jit(solution)/shard_map/update/pallas_call | solution.py:451
